TPU v7x, 256 devices: a whole 4x4x8 slice. The times are simulated.
256 devices in a mesh: fsdp: 16 (over y, x), rep: 16 (over z, core).
Axes of the slice: x: 4, y: 4, z: 8, core: 2. Of those that a mesh axis runs over, the one named last changes fastest.
Arguments:
- grad_parts: bfloat16 [16, 8192, 4096], P('rep', 'fsdp'), may hold values from -170 to 170
- owner_table: int32 [32], replicated, may hold values from 0 to 31, each once
- left_stats: float32 [512, 256, 256], P(('fsdp', 'rep')), may hold values from -1e-05 to 1e-05, as said below
- right_stats: float32 [512, 256, 256], P(('fsdp', 'rep')), may hold values from -1e-05 to 1e-05, as said below
- accum: float32 [512, 256, 256], P(('fsdp', 'rep')), may hold values from 1e-08 to 1e-06
- master: float32 [512, 256, 256], P(('fsdp', 'rep')), may hold values from -1.5 to 1.5
Outputs:
- steps: float32 [512, 256, 256], P(('fsdp', 'rep'))
- weights_new: bfloat16 [8192, 4096], P('fsdp')
Inputs may be any that keep to these rules, and one draw needn't show every extreme that they name: owner_table is a permutation of the 32 local tile ids; the device at index r of rep owns the slots r * 2 to (r + 1) * 2 - 1 of its row band. `left_stats`: each slot's matrix is symmetric positive definite. `right_stats`: each slot's matrix is symmetric positive definite.
All inputs are finite; a program needn't handle non-finite values.
Results may differ from a plain program's by a relative error of at most 0.001.
Values may be sent and summed in bfloat16 or wider, within the bound.
A program may use at most 64 MiB of HBM per device.

v0:
```python
import functools
import jax
import jax.numpy as jnp
from jax import lax
from jax.experimental import pallas as pl
from jax.experimental.pallas import tpu as pltpu
from jax.sharding import PartitionSpec as P

ITERS = 8
EPSILON = 1e-06
STEP_RATE = 0.2
CLIP_NORM = 1.0
W = 256
LEVELS = 32767.0
TINY = 1e-30
f32, bf16, i16 = jnp.float32, jnp.bfloat16, jnp.int16
MESH = pl.DeviceIdType.MESH

OFFSETS = (4, -3, 3, -2, 2, -1, 1, 0)
RS_HOPS = (4, 3, 3, 2, 2, 1, 1)
AG_HOPS = (1, 1, 2, 2, 3, 3, 4)
PICK = ((0, 1, 0, 1, 0, 1, 0), (1, 0, 1, 0, 1, 0, 1))
SIGN = (-1, 1)


def split(x):
    high = x.astype(bf16)
    return high, (x - high.astype(f32)).astype(bf16)


def dot(a, b):
    return jnp.dot(a, b, preferred_element_type=f32)


def mm(a, b):
    return dot(a[0], b[0]) + (dot(a[0], b[1]) + dot(a[1], b[0]))


def gram_left(a):
    def one(u, v):
        return lax.dot_general(u, v, (((1,), (1,)), ((), ())), preferred_element_type=f32)

    return one(a[0], a[0]) + (one(a[0], a[1]) + one(a[1], a[0]))


def gram_right(a):
    def one(u, v):
        return lax.dot_general(u, v, (((0,), (0,)), ((), ())), preferred_element_type=f32)

    return one(a[0], a[0]) + (one(a[0], a[1]) + one(a[1], a[0]))


def eye():
    rows = lax.broadcasted_iota(jnp.int32, (W, W), 0)
    return (rows == lax.broadcasted_iota(jnp.int32, (W, W), 1)).astype(f32)


def spread(scale):
    tall = jnp.concatenate([scale] * 4, axis=0)
    return jnp.concatenate([tall, tall], axis=1)


def fold(x, op):
    parts = [x[8 * i : 8 * i + 8, :] for i in range(4)]
    both = op(op(parts[0], parts[1]), op(parts[2], parts[3]))
    return op(both[:, :128], both[:, 128:])


def kernel(
    table, band_h, left_h, right_h, accum_h, master_h,
    steps, gath,
    band, left, right, accum, master,
    stage, sib, total, sendq, sends, recvq, recvs, summed, ag, nsend, nrecv,
    mats, roots,
    in_sem, sib_ssem, sib_rsem, q_ssem, q_rsem, s_ssem, s_rsem,
    n_ssem, n_rsem, ag_ssem, ag_rsem, x_ssem, x_rsem, out_sem,
):
    f = lax.axis_index("fsdp")
    r = lax.axis_index("rep")
    z = r // 2
    c = r - 2 * z
    mate = {"rep": r + 1 - 2 * c}
    chips = 8

    def near(step):
        return {"rep": 2 * lax.rem(z + step + chips, chips) + c}

    def at(step):
        return lax.rem(z + step + chips, chips)

    barrier = pltpu.get_barrier_semaphore()
    for o in range(1, 16):
        pl.semaphore_signal(barrier, 1, device_id={"rep": lax.rem(r + o, 16)}, device_id_type=MESH)
        pl.semaphore_signal(barrier, 1, device_id={"fsdp": lax.rem(f + o, 16)}, device_id_type=MESH)

    loads = [
        pltpu.make_async_copy(
            band_h.at[pl.ds(W * (t // 16), W), pl.ds(W * (t % 16), W)], band.at[t], in_sem.at[0]
        )
        for t in range(32)
    ] + [
        pltpu.make_async_copy(left_h, left, in_sem.at[1]),
        pltpu.make_async_copy(right_h, right, in_sem.at[2]),
        pltpu.make_async_copy(accum_h, accum, in_sem.at[3]),
        pltpu.make_async_copy(master_h, master, in_sem.at[4]),
    ]
    for load in loads:
        load.start()
    pltpu.make_async_copy(band, band, in_sem.at[0]).wait()

    def to_mate(j):
        return pltpu.make_async_remote_copy(
            src_ref=stage.at[j], dst_ref=sib.at[j], send_sem=sib_ssem.at[j], recv_sem=sib_rsem.at[j],
            device_id=mate, device_id_type=MESH,
        )

    def fill(j):
        for k in range(2):
            ident = table[4 * at(OFFSETS[j]) + 2 * (1 - c) + k]
            stage[j, pl.ds(k * W, W), :] = band[ident]

    for j in range(8):
        fill(j)
        if j == 0:
            pl.semaphore_wait(barrier, 30)
        to_mate(j).start()

    def pair(j, k, i, ident):
        own = band[ident, pl.ds(32 * i, 32), :].astype(f32)
        return own + sib[j, pl.ds(k * W + 32 * i, 32), :].astype(f32)

    def arrived(d, m, i):
        return recvq[d, m, pl.ds(32 * i, 32), :].astype(f32) * spread(recvs[d, m])

    def data_copy(d, m):
        return pltpu.make_async_remote_copy(
            src_ref=sendq.at[d, m], dst_ref=recvq.at[d, m], send_sem=q_ssem.at[d, m], recv_sem=q_rsem.at[d, m],
            device_id=near(SIGN[d]), device_id_type=MESH,
        )

    def scale_copy(d, m):
        return pltpu.make_async_remote_copy(
            src_ref=sends.at[d, m], dst_ref=recvs.at[d, m], send_sem=s_ssem.at[d, m], recv_sem=s_rsem.at[d, m],
            device_id=near(SIGN[d]), device_id_type=MESH,
        )

    def message(d, m):
        j = OFFSETS.index(SIGN[d] * RS_HOPS[m]) if RS_HOPS[m] != 4 else 0
        k = PICK[d][m]
        ident = table[4 * at(OFFSETS[j]) + 2 * c + k]
        if m >= 2:
            data_copy(d, m - 2).wait_recv()
            scale_copy(d, m - 2).wait_recv()
        most = jnp.full((8, 128), TINY, f32)
        for i in range(8):
            x = pair(j, k, i, ident)
            if m >= 2:
                x = x + arrived(d, m - 2, i)
            total[d, pl.ds(32 * i, 32), :] = x
            most = jnp.maximum(most, fold(jnp.abs(x), jnp.maximum))
        sends[d, m] = most * (1.0 / LEVELS)
        inverse = spread(LEVELS / most)
        for i in range(8):
            x = total[d, pl.ds(32 * i, 32), :] * inverse
            sendq[d, m, pl.ds(32 * i, 32), :] = jnp.round(x).astype(jnp.int32).astype(i16)
        data_copy(d, m).start()
        scale_copy(d, m).start()

    waited = set()
    for m in range(7):
        for d in range(2):
            j = OFFSETS.index(SIGN[d] * RS_HOPS[m]) if RS_HOPS[m] != 4 else 0
            if j not in waited:
                to_mate(j).wait_recv()
                waited.add(j)
            message(d, m)
    to_mate(7).wait_recv()
    for d in range(2):
        for m in (5, 6):
            data_copy(d, m).wait_recv()
            scale_copy(d, m).wait_recv()
    size = jnp.zeros((8, 128), f32)
    for k in range(2):
        ident = table[4 * z + 2 * c + k]
        for i in range(8):
            x = pair(7, k, i, ident)
            for d in range(2):
                m = 5 if PICK[d][5] == k else 6
                x = x + arrived(d, m, i)
            summed[k, pl.ds(32 * i, 32), :] = x
            size = size + fold(x * x, jnp.add)

    def norm_copy(stg, o):
        peer = {"rep": lax.rem(r + o, 16)} if stg == 0 else {"fsdp": lax.rem(f + o, 16)}
        return pltpu.make_async_remote_copy(
            src_ref=nsend.at[stg], dst_ref=nrecv.at[stg, o - 1], send_sem=n_ssem.at[stg], recv_sem=n_rsem.at[stg],
            device_id=peer, device_id_type=MESH,
        )

    def norm_all(stg):
        return pltpu.make_async_copy(nrecv.at[stg], nrecv.at[stg], n_rsem.at[stg])

    nsend[0] = size
    for o in range(1, 16):
        norm_copy(0, o).start()

    for load in loads[32:]:
        load.wait()
    for k in range(2):
        parts = split(summed[k])
        mats[2 * k] = gram_left(parts)
        mats[2 * k + 1] = gram_right(parts)

    norm_all(0).wait()
    for o in range(15):
        size = size + nrecv[0, o]
    nsend[1] = size
    for o in range(1, 16):
        norm_copy(1, o).start()
    norm_all(1).wait()
    for o in range(15):
        size = size + nrecv[1, o]
    norm_sq = jnp.sum(size, keepdims=True)
    clip = jnp.minimum(1.0, CLIP_NORM / (jnp.sqrt(norm_sq) + EPSILON))

    ident = eye()
    for k in range(2):
        for s in range(2):
            stats = left if s == 0 else right
            t = 2 * k + s
            a = stats[k] + (clip * clip) * mats[t] + EPSILON * ident
            zeta = 2.5 / jnp.sqrt(jnp.sum(a * a, keepdims=True))
            cur = zeta * a
            p = 1.25 * ident - 0.25 * cur
            roots[t] = jnp.sqrt(jnp.sqrt(zeta)) * p
            ps = split(p)
            ss = split(mm(ps, ps))
            qs = split(mm(ss, ss))
            mats[t] = mm(qs, split(cur))

    def sweep(i, carry):
        curs = [mats[t] for t in range(4)]
        pss = [split(1.25 * ident - 0.25 * cur) for cur in curs]
        for t in range(4):
            roots[t] = mm(split(roots[t]), pss[t])
        sss = [split(mm(p, p)) for p in pss]
        qss = [split(mm(s, s)) for s in sss]
        for t in range(4):
            mats[t] = mm(qss[t], split(curs[t]))
        return carry

    lax.fori_loop(0, ITERS - 2, sweep, 0)
    for t in range(4):
        p = 1.25 * ident - 0.25 * mats[t]
        roots[t] = mm(split(roots[t]), split(p))

    for k in range(2):
        g = clip * summed[k]
        sham = mm(split(mm(split(roots[2 * k]), split(g))), split(roots[2 * k + 1]))
        ada = g / (jnp.sqrt(accum[k] + g * g) + EPSILON)
        ada_size = jnp.sqrt(jnp.sum(ada * ada, keepdims=True))
        sham_size = jnp.sqrt(jnp.sum(sham * sham, keepdims=True))
        step = sham * (ada_size / (sham_size + EPSILON))
        steps[k] = step
        ag[4 * z + 2 * c + k] = (master[k] - STEP_RATE * step).astype(bf16)

    def slot_of(d, m, back):
        origin = at(-SIGN[d] * (AG_HOPS[m] - back))
        return 4 * origin + 2 * c + PICK[d][m]

    def ag_copy(d, m):
        slot = slot_of(d, m, 1)
        return pltpu.make_async_remote_copy(
            src_ref=ag.at[slot], dst_ref=ag.at[slot], send_sem=ag_ssem.at[d, m], recv_sem=ag_rsem.at[d, m],
            device_id=near(SIGN[d]), device_id_type=MESH,
        )

    def ag_recv(d, m):
        slot = slot_of(d, m, 0)
        return pltpu.make_async_remote_copy(
            src_ref=ag.at[slot], dst_ref=ag.at[slot], send_sem=ag_ssem.at[d, m], recv_sem=ag_rsem.at[d, m],
            device_id=near(SIGN[d]), device_id_type=MESH,
        )

    def mate_copy(n, slot):
        return pltpu.make_async_remote_copy(
            src_ref=ag.at[slot], dst_ref=gath.at[slot], send_sem=x_ssem.at[n], recv_sem=x_rsem.at[n],
            device_id=mate, device_id_type=MESH,
        )

    def out_copy(n, slot):
        return pltpu.make_async_copy(ag.at[slot], gath.at[slot], out_sem.at[n])

    for m in range(2):
        for d in range(2):
            ag_copy(d, m).start()
    moves = []
    for k in range(2):
        moves.append((k, 4 * z + 2 * c + k))
        mate_copy(*moves[-1]).start()
        out_copy(*moves[-1]).start()
    for m in range(7):
        for d in range(2):
            ag_recv(d, m).wait_recv()
            if m + 2 < 7:
                ag_copy(d, m + 2).start()
            moves.append((2 + 2 * m + d, slot_of(d, m, 0)))
            mate_copy(*moves[-1]).start()
            out_copy(*moves[-1]).start()

    for move in moves:
        out_copy(*move).wait()
        mate_copy(*move).wait_send()
        mate_copy(*move).wait_recv()
    for d in range(2):
        for m in range(7):
            ag_copy(d, m).wait_send()
            data_copy(d, m).wait_send()
            scale_copy(d, m).wait_send()
    for j in range(8):
        to_mate(j).wait_send()
    for stg in range(2):
        norm_all_sent = pltpu.make_async_copy(nrecv.at[stg], nrecv.at[stg], n_ssem.at[stg])
        norm_all_sent.wait()


def place(table, gath, steps_in, weights, steps, sems):
    copies = [pltpu.make_async_copy(steps_in, steps, sems.at[32])]
    for s in range(32):
        ident = table[s]
        top = pl.multiple_of((ident // 16) * W, W)
        lead = pl.multiple_of((ident % 16) * W, W)
        copies.append(
            pltpu.make_async_copy(gath.at[s], weights.at[pl.ds(top, W), pl.ds(lead, W)], sems.at[s])
        )
    for copy in copies:
        copy.start()
    for copy in copies:
        copy.wait()


def per_device(grad_parts, owner_table, left_stats, right_stats, accum, master):
    band = grad_parts[0]
    smem = pl.BlockSpec(memory_space=pltpu.SMEM)
    anyw = pl.BlockSpec(memory_space=pl.ANY)
    vmem = pl.BlockSpec(memory_space=pltpu.VMEM)
    tiles = (2, W, W)
    dma = pltpu.SemaphoreType.DMA
    steps, gath = pl.pallas_call(
        kernel,
        out_shape=(
            jax.ShapeDtypeStruct(tiles, f32),
            jax.ShapeDtypeStruct((32, W, W), bf16),
        ),
        in_specs=[smem] + [anyw] * 5,
        out_specs=(vmem, anyw),
        scratch_shapes=[
            pltpu.VMEM((32, W, W), bf16),
            pltpu.VMEM(tiles, f32),
            pltpu.VMEM(tiles, f32),
            pltpu.VMEM(tiles, f32),
            pltpu.VMEM(tiles, f32),
            pltpu.VMEM((8, 2 * W, W), bf16),
            pltpu.VMEM((8, 2 * W, W), bf16),
            pltpu.VMEM(tiles, f32),
            pltpu.VMEM((2, 7, W, W), i16),
            pltpu.VMEM((2, 7, 8, 128), f32),
            pltpu.VMEM((2, 7, W, W), i16),
            pltpu.VMEM((2, 7, 8, 128), f32),
            pltpu.VMEM(tiles, f32),
            pltpu.VMEM((32, W, W), bf16),
            pltpu.VMEM((2, 8, 128), f32),
            pltpu.VMEM((2, 15, 8, 128), f32),
            pltpu.VMEM((4, W, W), f32),
            pltpu.VMEM((4, W, W), f32),
            dma((5,)), dma((8,)), dma((8,)), dma((2, 7)), dma((2, 7)), dma((2, 7)), dma((2, 7)),
            dma((2,)), dma((2,)), dma((2, 7)), dma((2, 7)), dma((16,)), dma((16,)), dma((16,)),
        ],
        compiler_params=pltpu.CompilerParams(
            collective_id=0, has_side_effects=True, vmem_limit_bytes=56 << 20
        ),
        name="shampoo",
    )(owner_table, band, left_stats, right_stats, accum, master)
    weights, steps = pl.pallas_call(
        place,
        out_shape=(
            jax.ShapeDtypeStruct(band.shape, bf16),
            jax.ShapeDtypeStruct(tiles, f32),
        ),
        in_specs=[smem, anyw, anyw],
        out_specs=(anyw, anyw),
        scratch_shapes=[dma((33,))],
        compiler_params=pltpu.CompilerParams(vmem_limit_bytes=56 << 20),
        name="place",
    )(owner_table, gath, steps)
    return (steps, weights)


def solution(mesh):
    return jax.shard_map(
        per_device,
        mesh=mesh,
        in_specs=(
            P("rep", "fsdp", None),
            P(),
            P(("fsdp", "rep"), None, None),
            P(("fsdp", "rep"), None, None),
            P(("fsdp", "rep"), None, None),
            P(("fsdp", "rep"), None, None),
        ),
        out_specs=(P(("fsdp", "rep"), None, None), P("fsdp", None)),
        check_vma=False,
    )
```

profile of v0, /device:TPU:1, one launch (start us, length us, event | category | flops | bytes accessed | tf_op | source)
XLA Modules:
  0.0 233.5 jit_solution(8875103944045371235)
XLA Ops:
  0.6 87.8 %shampoo.1 = (f32[2,256,256]{2,1,0:T(8,128)}, bf16[32,256,256]{2,1,0:T(8,128)(2,1)}) custom-call(s32[32]{0:T(128)} %table.3, bf16[512,4096]{1,0:T(8,128)(2,1)} %bitcast.1, f32[2,256,256]{2,1,0:T(8,128)} %left_h.1, f32[2,256,256]{2,1,0:T(8,128)} %right_h.1, f32[2,256,256]{2,1,0:T(8,128)} %accum_h.1, f32[2,256,256]{2,1,0:T(8,128)} %master_h.1), custom_call_target="tpu_custom_call" | custom-call | tf_op jit(solution)/shard_map/shampoo/pallas_call | solution.py:349
  88.5 145.0 %place.1 = (bf16[512,4096]{1,0:T(8,128)(2,1)}, f32[2,256,256]{2,1,0:T(8,128)}) custom-call(s32[32]{0:T(128)} %table.3, bf16[32,256,256]{2,1,0:T(8,128)(2,1)} %get-tuple-element.6.gath, f32[2,256,256]{2,1,0:T(8,128)} %get-tuple-element.7.steps_in), custom_call_target="tpu_custom_call" | custom-call | tf_op jit(solution)/shard_map/place/pallas_call | solution.py:384
where the time goes:
time: 234 us; the launch traced here: 233 us
  Pallas kernels  233 us (100%)
    pallas_call x1, Pallas kernels, per_device(): pl.pallas_call(place, out_shape=(jax.ShapeDtypeStruct(band.shape, bf16),...  145 us
    pallas_call x1, Pallas kernels, per_device(): pl.pallas_call(kernel, out_shape=(jax.ShapeDtypeStruct(tiles, f32), jax.S...  87.8 us

commit v1 on v0

--- a/solution.py
+++ b/solution.py
@@ -68,12 +68,12 @@
 
 def kernel(
     table, band_h, left_h, right_h, accum_h, master_h,
-    steps, gath,
+    steps, ag,
     band, left, right, accum, master,
-    stage, sib, total, sendq, sends, recvq, recvs, summed, ag, nsend, nrecv,
+    stage, sib, total, sendq, sends, recvq, recvs, summed, nsend, nrecv,
     mats, roots,
     in_sem, sib_ssem, sib_rsem, q_ssem, q_rsem, s_ssem, s_rsem,
-    n_ssem, n_rsem, ag_ssem, ag_rsem, x_ssem, x_rsem, out_sem,
+    n_ssem, n_rsem, ag_ssem, ag_rsem, x_ssem, x_rsem,
 ):
     f = lax.axis_index("fsdp")
     r = lax.axis_index("rep")
@@ -284,12 +284,9 @@
 
     def mate_copy(n, slot):
         return pltpu.make_async_remote_copy(
-            src_ref=ag.at[slot], dst_ref=gath.at[slot], send_sem=x_ssem.at[n], recv_sem=x_rsem.at[n],
+            src_ref=ag.at[slot], dst_ref=ag.at[slot], send_sem=x_ssem.at[n], recv_sem=x_rsem.at[n],
             device_id=mate, device_id_type=MESH,
         )
-
-    def out_copy(n, slot):
-        return pltpu.make_async_copy(ag.at[slot], gath.at[slot], out_sem.at[n])
 
     for m in range(2):
         for d in range(2):
@@ -298,7 +295,6 @@
     for k in range(2):
         moves.append((k, 4 * z + 2 * c + k))
         mate_copy(*moves[-1]).start()
-        out_copy(*moves[-1]).start()
     for m in range(7):
         for d in range(2):
             ag_recv(d, m).wait_recv()
@@ -306,10 +302,8 @@
                 ag_copy(d, m + 2).start()
             moves.append((2 + 2 * m + d, slot_of(d, m, 0)))
             mate_copy(*moves[-1]).start()
-            out_copy(*moves[-1]).start()
 
     for move in moves:
-        out_copy(*move).wait()
         mate_copy(*move).wait_send()
         mate_copy(*move).wait_recv()
     for d in range(2):
@@ -348,12 +342,9 @@
     dma = pltpu.SemaphoreType.DMA
     steps, gath = pl.pallas_call(
         kernel,
-        out_shape=(
-            jax.ShapeDtypeStruct(tiles, f32),
-            jax.ShapeDtypeStruct((32, W, W), bf16),
-        ),
-        in_specs=[smem] + [anyw] * 5,
-        out_specs=(vmem, anyw),
+        out_shape=(pltpu.VMEM(tiles, f32), pltpu.VMEM((32, W, W), bf16)),
+        in_specs=[smem] + [pl.BlockSpec(memory_space=pltpu.HBM)] * 5,
+        out_specs=(vmem, vmem),
         scratch_shapes=[
             pltpu.VMEM((32, W, W), bf16),
             pltpu.VMEM(tiles, f32),
@@ -368,16 +359,15 @@
             pltpu.VMEM((2, 7, W, W), i16),
             pltpu.VMEM((2, 7, 8, 128), f32),
             pltpu.VMEM(tiles, f32),
-            pltpu.VMEM((32, W, W), bf16),
             pltpu.VMEM((2, 8, 128), f32),
             pltpu.VMEM((2, 15, 8, 128), f32),
             pltpu.VMEM((4, W, W), f32),
             pltpu.VMEM((4, W, W), f32),
             dma((5,)), dma((8,)), dma((8,)), dma((2, 7)), dma((2, 7)), dma((2, 7)), dma((2, 7)),
-            dma((2,)), dma((2,)), dma((2, 7)), dma((2, 7)), dma((16,)), dma((16,)), dma((16,)),
+            dma((2,)), dma((2,)), dma((2, 7)), dma((2, 7)), dma((16,)), dma((16,)),
         ],
         compiler_params=pltpu.CompilerParams(
-            collective_id=0, has_side_effects=True, vmem_limit_bytes=56 << 20
+            collective_id=0, has_side_effects=True, vmem_limit_bytes=58 << 20
         ),
         name="shampoo",
     )(owner_table, band, left_stats, right_stats, accum, master)
@@ -387,10 +377,10 @@
             jax.ShapeDtypeStruct(band.shape, bf16),
             jax.ShapeDtypeStruct(tiles, f32),
         ),
-        in_specs=[smem, anyw, anyw],
+        in_specs=[smem, vmem, vmem],
         out_specs=(anyw, anyw),
         scratch_shapes=[dma((33,))],
-        compiler_params=pltpu.CompilerParams(vmem_limit_bytes=56 << 20),
+        compiler_params=pltpu.CompilerParams(vmem_limit_bytes=16 << 20),
         name="place",
     )(owner_table, gath, steps)
     return (steps, weights)

time: 234 us -> 90.5 us (0.39)
  Pallas kernels: 233 us -> 89.7 us
    pallas_call x1, Pallas kernels: 145 us -> 2.97 us  [per_device(): pl.pallas_call(place, out_shape=(jax.ShapeDtypeStruct(band.shape, bf16),...]
where the time goes in v1:
time: 90.5 us; the launch traced here: 90.4 us
  Pallas kernels  89.7 us (99%)
    pallas_call x1, Pallas kernels, per_device(): pl.pallas_call(kernel, out_shape=(pltpu.VMEM(tiles, f32), pltpu.VMEM((32,...  86.7 us
    pallas_call x1, Pallas kernels, per_device(): pl.pallas_call(place, out_shape=(jax.ShapeDtypeStruct(band.shape, bf16),...  2.97 us

profile of v1, /device:TPU:1, one launch (start us, length us, event | category | flops | bytes accessed | tf_op | source)
XLA Modules:
  0.0 90.4 jit_solution(18269185374048334690)
XLA Ops:
  0.6 0.0 copy-start
  0.6 86.7 %shampoo.1 = (f32[2,256,256]{2,1,0:T(8,128)S(1)}, bf16[32,256,256]{2,1,0:T(8,128)(2,1)S(1)}) custom-call(s32[32]{0:T(128)} %table.3, bf16[512,4096]{1,0:T(8,128)(2,1)} %bitcast.1, f32[2,256,256]{2,1,0:T(8,128)} %left_h.1, f32[2,256,256]{2,1,0:T(8,128)} %right_h.1, f32[2,256,256]{2,1,0:T(8,128)} %accum_h.1, f32[2,256,256]{2,1,0:T(8,128)} %master_h.1), custom_call_target="tpu_custom_call" | custom-call | tf_op jit(solution)/shard_map/shampoo/pallas_call | solution.py:343
  87.4 0.0 copy-done
  87.4 3.0 %place.1 = (bf16[512,4096]{1,0:T(8,128)(2,1)}, f32[2,256,256]{2,1,0:T(8,128)}) custom-call(s32[32]{0:T(128)S(1)} %copy-done, bf16[32,256,256]{2,1,0:T(8,128)(2,1)S(1)} %get-tuple-element.6.gath, f32[2,256,256]{2,1,0:T(8,128)S(1)} %get-tuple-element.7.steps_in), custom_call_target="tpu_custom_call" | custom-call | tf_op jit(solution)/shard_map/place/pallas_call | solution.py:374
Async XLA Ops:
  0.6 86.8 %copy-start = (s32[32]{0:T(128)S(1)}, s32[32]{0:T(128)}, u32[]{:S(2)}) copy-start(s32[32]{0:T(128)} %table.3) | copy-start | bytes 388

commit v2 on v1

v2 whole, which is shorter than its diff:
```python
import functools
import jax
import jax.numpy as jnp
from jax import lax
from jax.experimental import pallas as pl
from jax.experimental.pallas import tpu as pltpu
from jax.sharding import PartitionSpec as P

ITERS = 8
EPSILON = 1e-06
STEP_RATE = 0.2
CLIP_NORM = 1.0
W = 256
LEVELS = 32767.0
TINY = 1e-30
f32, bf16, i16 = jnp.float32, jnp.bfloat16, jnp.int16
MESH = pl.DeviceIdType.MESH

RS_ORDER = ((4, 0), (3, 1), (3, 0), (2, 1), (2, 0), (1, 1), (1, 0), (0, 0))
AG_ORDER = ((1, 0), (1, 1), (2, 0), (2, 1), (3, 0), (3, 1), (4, 0))


def split(x):
    high = x.astype(bf16)
    return high, (x - high.astype(f32)).astype(bf16)


def dot(a, b):
    return jnp.dot(a, b, preferred_element_type=f32)


def mm(a, b):
    return dot(a[0], b[0]) + (dot(a[0], b[1]) + dot(a[1], b[0]))


def gram_left(a):
    def one(u, v):
        return lax.dot_general(u, v, (((1,), (1,)), ((), ())), preferred_element_type=f32)

    return one(a[0], a[0]) + (one(a[0], a[1]) + one(a[1], a[0]))


def gram_right(a):
    def one(u, v):
        return lax.dot_general(u, v, (((0,), (0,)), ((), ())), preferred_element_type=f32)

    return one(a[0], a[0]) + (one(a[0], a[1]) + one(a[1], a[0]))


def eye():
    rows = lax.broadcasted_iota(jnp.int32, (W, W), 0)
    return (rows == lax.broadcasted_iota(jnp.int32, (W, W), 1)).astype(f32)


def spread(scale):
    return jnp.broadcast_to(jnp.concatenate([scale, scale], axis=1), (32, W))


def fold(x, op):
    parts = [x[8 * i : 8 * i + 8, :] for i in range(4)]
    both = op(op(parts[0], parts[1]), op(parts[2], parts[3]))
    return op(both[:, :128], both[:, 128:])


def kernel(
    table, band_h, left_h, right_h, accum_h, master_h,
    steps, ag,
    band, left, right, accum, master,
    stage, sib, total, sendq, sends, recvq, recvs, summed, nsend, nrecv,
    mats, roots,
    in_sem, sib_ssem, sib_rsem, q_ssem, q_rsem, s_ssem, s_rsem,
    n_ssem, n_rsem, ag_ssem, ag_rsem, x_ssem, x_rsem, own_rsem,
):
    f = lax.axis_index("fsdp")
    r = lax.axis_index("rep")
    z = r // 2
    c = r - 2 * z
    mate = {"rep": r + 1 - 2 * c}
    once = jnp.minimum(r + 1, 1)

    def block(work):
        def body(i, carry):
            work()
            return carry

        lax.fori_loop(0, once, body, 0)

    chips = 8

    way = 2 * c - 1

    def chip(hops):
        return lax.rem(z + way * hops + chips, chips)

    def core(other):
        return 1 - c if other else c

    loads = [
        pltpu.make_async_copy(
            band_h.at[pl.ds(W * (t // 16), W), pl.ds(W * (t % 16), W)], band.at[t], in_sem.at[0]
        )
        for t in range(32)
    ] + [
        pltpu.make_async_copy(left_h, left, in_sem.at[1]),
        pltpu.make_async_copy(right_h, right, in_sem.at[2]),
        pltpu.make_async_copy(accum_h, accum, in_sem.at[3]),
        pltpu.make_async_copy(master_h, master, in_sem.at[4]),
    ]
    for load in loads:
        load.start()
    barrier = pltpu.get_barrier_semaphore()
    for o in range(1, 16):
        pl.semaphore_signal(barrier, 1, device_id={"rep": lax.rem(r + o, 16)}, device_id_type=MESH)
        pl.semaphore_signal(barrier, 1, device_id={"fsdp": lax.rem(f + o, 16)}, device_id_type=MESH)

    pltpu.make_async_copy(band, band, in_sem.at[0]).wait()

    def to_mate(j):
        return pltpu.make_async_remote_copy(
            src_ref=stage.at[j], dst_ref=sib.at[j], send_sem=sib_ssem, recv_sem=sib_rsem.at[j],
            device_id=mate, device_id_type=MESH,
        )

    def fill(j):
        hops, other = RS_ORDER[j]
        for k in range(2):
            stage[j, pl.ds(k * W, W), :] = band[table[4 * chip(-hops) + 2 * core(1 - other) + k]]

    for j in range(8):
        fill(j)
        if j == 0:
            pl.semaphore_wait(barrier, 30)
        to_mate(j).start()

    def pair(j, k, i, ident):
        own = band[ident, pl.ds(32 * i, 32), :].astype(f32)
        return own + sib[j, pl.ds(k * W + 32 * i, 32), :].astype(f32)

    def arrived(j, k, i):
        return recvq[j, k, pl.ds(32 * i, 32), :].astype(f32) * spread(recvs[j, k])

    def ahead(j):
        return {"rep": 2 * chip(1) + (core(RS_ORDER[j][1]) if RS_ORDER[j][0] == 1 else c)}

    def data_copy(j, k):
        return pltpu.make_async_remote_copy(
            src_ref=sendq.at[j, k], dst_ref=recvq.at[j, k], send_sem=q_ssem, recv_sem=q_rsem.at[j, k],
            device_id=ahead(j), device_id_type=MESH,
        )

    def scale_copy(j, k):
        return pltpu.make_async_remote_copy(
            src_ref=sends.at[j, k], dst_ref=recvs.at[j, k], send_sem=s_ssem.at[j, k], recv_sem=s_rsem.at[j, k],
            device_id=ahead(j), device_id_type=MESH,
        )

    def message(j, k):
        hops, other = RS_ORDER[j]
        ident = table[4 * chip(hops) + 2 * core(other) + k]
        if j >= 2:
            data_copy(j - 2, k).wait_recv()
            scale_copy(j - 2, k).wait_recv()
        most = jnp.full((8, 128), TINY, f32)
        for i in range(8):
            x = pair(j, k, i, ident)
            if j >= 2:
                x = x + arrived(j - 2, k, i)
            total[k, pl.ds(32 * i, 32), :] = x
            most = jnp.maximum(most, fold(jnp.abs(x), jnp.maximum))
        most = jnp.max(most, axis=0, keepdims=True)
        sends[j, k] = most * (1.0 / LEVELS)
        inverse = spread(LEVELS / most)
        for i in range(8):
            x = total[k, pl.ds(32 * i, 32), :] * inverse
            sendq[j, k, pl.ds(32 * i, 32), :] = jnp.round(x).astype(jnp.int32).astype(i16)
        data_copy(j, k).start()
        scale_copy(j, k).start()

    for j in range(7):
        to_mate(j).wait_recv()
        for k in range(2):
            message(j, k)
    to_mate(7).wait_recv()
    size = jnp.zeros((8, 128), f32)
    for k in range(2):
        ident = table[4 * z + 2 * c + k]
        for j in (5, 6):
            data_copy(j, k).wait_recv()
            scale_copy(j, k).wait_recv()
        for i in range(8):
            x = pair(7, k, i, ident) + arrived(5, k, i) + arrived(6, k, i)
            summed[k, pl.ds(32 * i, 32), :] = x
            size = size + fold(x * x, jnp.add)

    def norm_copy(stg, o):
        peer = {"rep": lax.rem(r + o, 16)} if stg == 0 else {"fsdp": lax.rem(f + o, 16)}
        return pltpu.make_async_remote_copy(
            src_ref=nsend.at[stg], dst_ref=nrecv.at[stg, o - 1], send_sem=n_ssem.at[stg], recv_sem=n_rsem.at[stg],
            device_id=peer, device_id_type=MESH,
        )

    def norm_all(stg):
        return pltpu.make_async_copy(nrecv.at[stg], nrecv.at[stg], n_rsem.at[stg])

    nsend[0] = size
    for o in range(1, 16):
        norm_copy(0, o).start()

    for load in loads[32:]:
        load.wait()

    def left_grams():
        for k in range(2):
            mats[2 * k] = gram_left(split(summed[k]))

    def right_grams():
        for k in range(2):
            mats[2 * k + 1] = gram_right(split(summed[k]))

    block(left_grams)
    norm_all(0).wait()
    for o in range(15):
        size = size + nrecv[0, o]
    nsend[1] = size
    for o in range(1, 16):
        norm_copy(1, o).start()
    block(right_grams)
    norm_all(1).wait()
    for o in range(15):
        size = size + nrecv[1, o]
    norm_sq = jnp.sum(size, keepdims=True)
    clip = jnp.minimum(1.0, CLIP_NORM / (jnp.sqrt(norm_sq) + EPSILON))

    ident = eye()
    for k in range(2):
        for s in range(2):
            stats = left if s == 0 else right
            t = 2 * k + s
            a = stats[k] + (clip * clip) * mats[t] + EPSILON * ident
            zeta = 2.5 / jnp.sqrt(jnp.sum(a * a, keepdims=True))
            cur = zeta * a
            p = 1.25 * ident - 0.25 * cur
            roots[t] = jnp.sqrt(jnp.sqrt(zeta)) * p
            ps = split(p)
            ss = split(mm(ps, ps))
            mats[t] = mm(split(mm(ss, split(cur))), ss)

    for _ in range(ITERS - 2):
        curs = [mats[t] for t in range(4)]
        pss = [split(1.25 * ident - 0.25 * cur) for cur in curs]
        sss = [split(mm(p, p)) for p in pss]
        for t in range(4):
            roots[t] = mm(split(roots[t]), pss[t])
        uss = [split(mm(p, split(cur))) for p, cur in zip(sss, curs)]
        for t in range(4):
            mats[t] = mm(uss[t], sss[t])

    def last_roots(k):
        for t in (2 * k, 2 * k + 1):
            p = 1.25 * ident - 0.25 * mats[t]
            roots[t] = mm(split(roots[t]), split(p))

    def finish(k):
        g = clip * summed[k]
        sham = mm(split(mm(split(roots[2 * k]), split(g))), split(roots[2 * k + 1]))
        ada = g / (jnp.sqrt(accum[k] + g * g) + EPSILON)
        ada_size = jnp.sqrt(jnp.sum(ada * ada, keepdims=True))
        sham_size = jnp.sqrt(jnp.sum(sham * sham, keepdims=True))
        step = sham * (ada_size / (sham_size + EPSILON))
        steps[k] = step
        ag[4 * z + 2 * c + k] = (master[k] - STEP_RATE * step).astype(bf16)

    def ag_copy(i, k, back=1):
        hops, other = AG_ORDER[i]
        slot = 4 * chip(back - hops) + 2 * core(other) + k
        return pltpu.make_async_remote_copy(
            src_ref=ag.at[slot], dst_ref=ag.at[slot], send_sem=ag_ssem, recv_sem=ag_rsem.at[i, k],
            device_id={"rep": 2 * chip(1) + c}, device_id_type=MESH,
        )

    def share(i, k):
        hops, other = AG_ORDER[i]
        slot = 4 * chip(-hops) + 2 * core(other) + k
        return pltpu.make_async_remote_copy(
            src_ref=ag.at[slot], dst_ref=ag.at[slot], send_sem=x_ssem, recv_sem=x_rsem,
            device_id=mate, device_id_type=MESH,
        )

    def own_share(k):
        slot = 4 * z + 2 * c + k
        return pltpu.make_async_remote_copy(
            src_ref=ag.at[slot], dst_ref=ag.at[slot], send_sem=x_ssem, recv_sem=own_rsem.at[k],
            device_id=mate, device_id_type=MESH,
        )

    def own_out(k):
        ag_copy(0, k).start()
        own_share(k).start()

    def mate_out(k):
        own_share(k).wait_recv()
        ag_copy(1, k).start()

    last_roots(0)
    finish(0)
    own_out(0)
    block(lambda: last_roots(1))
    mate_out(0)
    block(lambda: finish(1))
    own_out(1)
    mate_out(1)
    for i in range(7):
        for k in range(2):
            ag_copy(i, k, 0).wait_recv()
            if i + 2 < 7:
                ag_copy(i + 2, k).start()
            share(i, k).start()

    def drain(ref, sem):
        pltpu.make_async_copy(ref, ref, sem).wait()

    drain(stage, sib_ssem)
    drain(sendq, q_ssem)
    drain(ag.at[pl.ds(0, 14)], ag_ssem)
    drain(ag.at[pl.ds(0, 16)], x_ssem)
    for j in range(7):
        for k in range(2):
            scale_copy(j, k).wait_send()
    for stg in range(2):
        drain(nrecv.at[stg], n_ssem.at[stg])
    drain(ag.at[pl.ds(0, 14)], x_rsem)


def place(table, gath, steps_in, weights, steps, sems):
    for s in range(32):
        ident = table[s]
        top = pl.multiple_of((ident // 16) * W, W)
        lead = pl.multiple_of((ident % 16) * W, W)
        pltpu.make_async_copy(gath.at[s], weights.at[pl.ds(top, W), pl.ds(lead, W)], sems.at[0]).start()
    keep = pltpu.make_async_copy(steps_in, steps, sems.at[1])
    keep.start()
    pltpu.make_async_copy(gath, gath, sems.at[0]).wait()
    keep.wait()


def per_device(grad_parts, owner_table, left_stats, right_stats, accum, master):
    band = grad_parts[0]
    smem = pl.BlockSpec(memory_space=pltpu.SMEM)
    anyw = pl.BlockSpec(memory_space=pl.ANY)
    vmem = pl.BlockSpec(memory_space=pltpu.VMEM)
    tiles = (2, W, W)
    dma = pltpu.SemaphoreType.DMA
    steps, gath = pl.pallas_call(
        kernel,
        out_shape=(pltpu.VMEM(tiles, f32), pltpu.VMEM((32, W, W), bf16)),
        in_specs=[smem] + [pl.BlockSpec(memory_space=pltpu.HBM)] * 5,
        out_specs=(vmem, vmem),
        scratch_shapes=[
            pltpu.VMEM((32, W, W), bf16),
            pltpu.VMEM(tiles, f32),
            pltpu.VMEM(tiles, f32),
            pltpu.VMEM(tiles, f32),
            pltpu.VMEM(tiles, f32),
            pltpu.VMEM((8, 2 * W, W), bf16),
            pltpu.VMEM((8, 2 * W, W), bf16),
            pltpu.VMEM(tiles, f32),
            pltpu.VMEM((7, 2, W, W), i16),
            pltpu.VMEM((7, 2, 1, 128), f32),
            pltpu.VMEM((7, 2, W, W), i16),
            pltpu.VMEM((7, 2, 1, 128), f32),
            pltpu.VMEM(tiles, f32),
            pltpu.VMEM((2, 8, 128), f32),
            pltpu.VMEM((2, 15, 8, 128), f32),
            pltpu.VMEM((4, W, W), f32),
            pltpu.VMEM((4, W, W), f32),
            dma((5,)), dma, dma((8,)), dma, dma((7, 2)), dma((7, 2)), dma((7, 2)),
            dma((2,)), dma((2,)), dma, dma((7, 2)), dma, dma, dma((2,)),
        ],
        compiler_params=pltpu.CompilerParams(
            collective_id=0, has_side_effects=True, vmem_limit_bytes=58 << 20
        ),
        name="shampoo",
    )(owner_table, band, left_stats, right_stats, accum, master)
    weights, steps = pl.pallas_call(
        place,
        out_shape=(
            jax.ShapeDtypeStruct(band.shape, bf16),
            jax.ShapeDtypeStruct(tiles, f32),
        ),
        in_specs=[smem, vmem, vmem],
        out_specs=(anyw, anyw),
        scratch_shapes=[dma((2,))],
        compiler_params=pltpu.CompilerParams(vmem_limit_bytes=16 << 20),
        name="place",
    )(owner_table, gath, steps)
    return (steps, weights)


def solution(mesh):
    return jax.shard_map(
        per_device,
        mesh=mesh,
        in_specs=(
            P("rep", "fsdp", None),
            P(),
            P(("fsdp", "rep"), None, None),
            P(("fsdp", "rep"), None, None),
            P(("fsdp", "rep"), None, None),
            P(("fsdp", "rep"), None, None),
        ),
        out_specs=(P(("fsdp", "rep"), None, None), P("fsdp", None)),
        check_vma=False,
    )
```

time: 90.5 us -> 86.4 us (0.955)
  Pallas kernels: 89.7 us -> 85.5 us
    pallas_call x1, Pallas kernels: 86.7 us -> 82.7 us  [per_device(): pl.pallas_call(kernel, out_shape=(pltpu.VMEM(tiles, f32), pltpu.VMEM((32,...]
where the time goes in v2:
time: 86.4 us; the launch traced here: 86.3 us
  Pallas kernels  85.5 us (99%)
    pallas_call x1, Pallas kernels, per_device(): pl.pallas_call(kernel, out_shape=(pltpu.VMEM(tiles, f32), pltpu.VMEM((32,...  82.7 us
    pallas_call x1, Pallas kernels, per_device(): pl.pallas_call(place, out_shape=(jax.ShapeDtypeStruct(band.shape, bf16),...  2.73 us

profile of v2, /device:TPU:1, one launch (start us, length us, event | category | flops | bytes accessed | tf_op | source)
XLA Modules:
  0.0 86.3 jit_solution(3843940575152558574)
XLA Ops:
  0.6 0.0 copy-start
  0.6 82.7 %shampoo.1 = (f32[2,256,256]{2,1,0:T(8,128)S(1)}, bf16[32,256,256]{2,1,0:T(8,128)(2,1)S(1)}) custom-call(s32[32]{0:T(128)} %table.3, bf16[512,4096]{1,0:T(8,128)(2,1)} %bitcast.1, f32[2,256,256]{2,1,0:T(8,128)} %left_h.1, f32[2,256,256]{2,1,0:T(8,128)} %right_h.1, f32[2,256,256]{2,1,0:T(8,128)} %accum_h.1, f32[2,256,256]{2,1,0:T(8,128)} %master_h.1), custom_call_target="tpu_custom_call" | custom-call | tf_op jit(solution)/shard_map/shampoo/pallas_call | solution.py:353
  83.4 0.0 copy-done
  83.4 2.7 %place.1 = (bf16[512,4096]{1,0:T(8,128)(2,1)}, f32[2,256,256]{2,1,0:T(8,128)}) custom-call(s32[32]{0:T(128)S(1)} %copy-done, bf16[32,256,256]{2,1,0:T(8,128)(2,1)S(1)} %get-tuple-element.6.gath, f32[2,256,256]{2,1,0:T(8,128)S(1)} %get-tuple-element.7.steps_in), custom_call_target="tpu_custom_call" | custom-call | tf_op jit(solution)/shard_map/place/pallas_call | solution.py:384
Async XLA Ops:
  0.6 82.8 %copy-start = (s32[32]{0:T(128)S(1)}, s32[32]{0:T(128)}, u32[]{:S(2)}) copy-start(s32[32]{0:T(128)} %table.3) | copy-start | bytes 388

commit v3 on v2

--- a/solution.py
+++ b/solution.py
@@ -63,12 +63,12 @@
 
 
 def kernel(
-    table, band_h, left_h, right_h, accum_h, master_h,
+    table_h, band_h, left_h, right_h, accum_h, master_h,
     steps, ag,
-    band, left, right, accum, master,
+    table, band, left, right, accum, master,
     stage, sib, total, sendq, sends, recvq, recvs, summed, nsend, nrecv,
     mats, roots,
-    in_sem, sib_ssem, sib_rsem, q_ssem, q_rsem, s_ssem, s_rsem,
+    in_sem, near_sem, sib_ssem, sib_rsem, q_ssem, q_rsem, s_ssem, s_rsem,
     n_ssem, n_rsem, ag_ssem, ag_rsem, x_ssem, x_rsem, own_rsem,
 ):
     f = lax.axis_index("fsdp")
@@ -106,14 +106,30 @@
         pltpu.make_async_copy(accum_h, accum, in_sem.at[3]),
         pltpu.make_async_copy(master_h, master, in_sem.at[4]),
     ]
-    for load in loads:
+    row = f - lax.rem(f, 4)
+    beside = [
+        {"fsdp": row + lax.rem(f + 1, 4)},
+        {"fsdp": row + lax.rem(f + 3, 4)},
+        {"fsdp": lax.rem(f + 4, 16)},
+        {"fsdp": lax.rem(f + 12, 16)},
+    ]
+    ring = [mate, {"rep": 2 * chip(1) + c}, {"rep": 2 * chip(-1) + c}, {"rep": 2 * chip(1) + 1 - c}]
+    barrier = pltpu.get_barrier_semaphore()
+    for peer in ring + beside:
+        pl.semaphore_signal(barrier, 1, device_id=peer, device_id_type=MESH)
+
+    def tell(turn):
+        for peer in beside:
+            pl.semaphore_signal(near_sem.at[turn], 1, device_id=peer, device_id_type=MESH)
+
+    fetch_table = pltpu.make_async_copy(table_h, table, in_sem.at[5])
+    fetch_table.start()
+    for load in loads[:32]:
         load.start()
-    barrier = pltpu.get_barrier_semaphore()
-    for o in range(1, 16):
-        pl.semaphore_signal(barrier, 1, device_id={"rep": lax.rem(r + o, 16)}, device_id_type=MESH)
-        pl.semaphore_signal(barrier, 1, device_id={"fsdp": lax.rem(f + o, 16)}, device_id_type=MESH)
-
+    fetch_table.wait()
     pltpu.make_async_copy(band, band, in_sem.at[0]).wait()
+    for load in loads[32:]:
+        load.start()
 
     def to_mate(j):
         return pltpu.make_async_remote_copy(
@@ -129,7 +145,7 @@
     for j in range(8):
         fill(j)
         if j == 0:
-            pl.semaphore_wait(barrier, 30)
+            pl.semaphore_wait(barrier, 8)
         to_mate(j).start()
 
     def pair(j, k, i, ident):
@@ -176,10 +192,16 @@
         data_copy(j, k).start()
         scale_copy(j, k).start()
 
+    tell(0)
     for j in range(7):
         to_mate(j).wait_recv()
         for k in range(2):
             message(j, k)
+        if j in (2, 4, 6):
+            turn = j // 2 - 1
+            pl.semaphore_wait(near_sem.at[turn], 4)
+            if turn < 2:
+                tell(turn + 1)
     to_mate(7).wait_recv()
     size = jnp.zeros((8, 128), f32)
     for k in range(2):
@@ -232,6 +254,11 @@
     clip = jnp.minimum(1.0, CLIP_NORM / (jnp.sqrt(norm_sq) + EPSILON))
 
     ident = eye()
+    fourths, factors = [], []
+
+    def advance(k, left_factor, right_factor):
+        roots[k] = mm(split(mm(left_factor, split(roots[k]))), right_factor)
+
     for k in range(2):
         for s in range(2):
             stats = left if s == 0 else right
@@ -240,29 +267,32 @@
             zeta = 2.5 / jnp.sqrt(jnp.sum(a * a, keepdims=True))
             cur = zeta * a
             p = 1.25 * ident - 0.25 * cur
-            roots[t] = jnp.sqrt(jnp.sqrt(zeta)) * p
+            fourths.append(jnp.sqrt(jnp.sqrt(zeta)))
             ps = split(p)
+            factors.append(ps)
             ss = split(mm(ps, ps))
             mats[t] = mm(split(mm(ss, split(cur))), ss)
+
+    for k in range(2):
+        roots[k] = (clip * fourths[2 * k] * fourths[2 * k + 1]) * summed[k]
+        advance(k, factors[2 * k], factors[2 * k + 1])
 
     for _ in range(ITERS - 2):
         curs = [mats[t] for t in range(4)]
         pss = [split(1.25 * ident - 0.25 * cur) for cur in curs]
         sss = [split(mm(p, p)) for p in pss]
-        for t in range(4):
-            roots[t] = mm(split(roots[t]), pss[t])
+        for k in range(2):
+            advance(k, pss[2 * k], pss[2 * k + 1])
         uss = [split(mm(p, split(cur))) for p, cur in zip(sss, curs)]
         for t in range(4):
             mats[t] = mm(uss[t], sss[t])
 
-    def last_roots(k):
-        for t in (2 * k, 2 * k + 1):
-            p = 1.25 * ident - 0.25 * mats[t]
-            roots[t] = mm(split(roots[t]), split(p))
+    def last_factors(k):
+        advance(k, *(split(1.25 * ident - 0.25 * mats[t]) for t in (2 * k, 2 * k + 1)))
 
     def finish(k):
         g = clip * summed[k]
-        sham = mm(split(mm(split(roots[2 * k]), split(g))), split(roots[2 * k + 1]))
+        sham = roots[k]
         ada = g / (jnp.sqrt(accum[k] + g * g) + EPSILON)
         ada_size = jnp.sqrt(jnp.sum(ada * ada, keepdims=True))
         sham_size = jnp.sqrt(jnp.sum(sham * sham, keepdims=True))
@@ -301,10 +331,10 @@
         own_share(k).wait_recv()
         ag_copy(1, k).start()
 
-    last_roots(0)
+    last_factors(0)
     finish(0)
     own_out(0)
-    block(lambda: last_roots(1))
+    block(lambda: last_factors(1))
     mate_out(0)
     block(lambda: finish(1))
     own_out(1)
@@ -353,9 +383,10 @@
     steps, gath = pl.pallas_call(
         kernel,
         out_shape=(pltpu.VMEM(tiles, f32), pltpu.VMEM((32, W, W), bf16)),
-        in_specs=[smem] + [pl.BlockSpec(memory_space=pltpu.HBM)] * 5,
+        in_specs=[pl.BlockSpec(memory_space=pltpu.HBM)] * 6,
         out_specs=(vmem, vmem),
         scratch_shapes=[
+            pltpu.SMEM((32,), jnp.int32),
             pltpu.VMEM((32, W, W), bf16),
             pltpu.VMEM(tiles, f32),
             pltpu.VMEM(tiles, f32),
@@ -372,8 +403,8 @@
             pltpu.VMEM((2, 8, 128), f32),
             pltpu.VMEM((2, 15, 8, 128), f32),
             pltpu.VMEM((4, W, W), f32),
-            pltpu.VMEM((4, W, W), f32),
-            dma((5,)), dma, dma((8,)), dma, dma((7, 2)), dma((7, 2)), dma((7, 2)),
+            pltpu.VMEM(tiles, f32),
+            dma((6,)), pltpu.SemaphoreType.REGULAR((3,)), dma, dma((8,)), dma, dma((7, 2)), dma((7, 2)), dma((7, 2)),
             dma((2,)), dma((2,)), dma, dma((7, 2)), dma, dma, dma((2,)),
         ],
         compiler_params=pltpu.CompilerParams(

time: 86.4 us -> 85.1 us (0.985)
  Pallas kernels: 85.5 us -> 84.1 us
    pallas_call x1, Pallas kernels: 82.7 us -> 81.4 us  [per_device(): pl.pallas_call(kernel, out_shape=(pltpu.VMEM(tiles, f32), pltpu.VMEM((32,...]
where the time goes in v3:
time: 85.1 us; the launch traced here: 85 us
  Pallas kernels  84.1 us (99%)
    pallas_call x1, Pallas kernels, per_device(): pl.pallas_call(kernel, out_shape=(pltpu.VMEM(tiles, f32), pltpu.VMEM((32,...  81.4 us
    pallas_call x1, Pallas kernels, per_device(): pl.pallas_call(place, out_shape=(jax.ShapeDtypeStruct(band.shape, bf16),...  2.73 us

profile of v3, /device:TPU:1, one launch (start us, length us, event | category | flops | bytes accessed | tf_op | source)
XLA Modules:
  0.0 85.0 jit_solution(13522694476288240299)
XLA Ops:
  0.6 0.0 copy-start
  0.6 81.4 %shampoo.1 = (f32[2,256,256]{2,1,0:T(8,128)S(1)}, bf16[32,256,256]{2,1,0:T(8,128)(2,1)S(1)}) custom-call(s32[32]{0:T(128)} %table.1, bf16[512,4096]{1,0:T(8,128)(2,1)} %bitcast.1, f32[2,256,256]{2,1,0:T(8,128)} %left_h.1, f32[2,256,256]{2,1,0:T(8,128)} %right_h.1, f32[2,256,256]{2,1,0:T(8,128)} %accum_h.1, f32[2,256,256]{2,1,0:T(8,128)} %master_h.1), custom_call_target="tpu_custom_call" | custom-call | tf_op jit(solution)/shard_map/shampoo/pallas_call | solution.py:383
  82.1 0.0 copy-done
  82.1 2.7 %place.1 = (bf16[512,4096]{1,0:T(8,128)(2,1)}, f32[2,256,256]{2,1,0:T(8,128)}) custom-call(s32[32]{0:T(128)S(1)} %copy-done, bf16[32,256,256]{2,1,0:T(8,128)(2,1)S(1)} %get-tuple-element.6.gath, f32[2,256,256]{2,1,0:T(8,128)S(1)} %get-tuple-element.7.steps_in), custom_call_target="tpu_custom_call" | custom-call | tf_op jit(solution)/shard_map/place/pallas_call | solution.py:415
Async XLA Ops:
  0.6 81.4 %copy-start = (s32[32]{0:T(128)S(1)}, s32[32]{0:T(128)}, u32[]{:S(2)}) copy-start(s32[32]{0:T(128)} %table.1) | copy-start | bytes 388

commit v4 on v3

--- a/solution.py
+++ b/solution.py
@@ -67,7 +67,7 @@
     steps, ag,
     table, band, left, right, accum, master,
     stage, sib, total, sendq, sends, recvq, recvs, summed, nsend, nrecv,
-    mats, roots,
+    mats, roots, frob,
     in_sem, near_sem, sib_ssem, sib_rsem, q_ssem, q_rsem, s_ssem, s_rsem,
     n_ssem, n_rsem, ag_ssem, ag_rsem, x_ssem, x_rsem, own_rsem,
 ):
@@ -239,6 +239,7 @@
         for k in range(2):
             mats[2 * k + 1] = gram_right(split(summed[k]))
 
+    ident = eye()
     block(left_grams)
     norm_all(0).wait()
     for o in range(15):
@@ -246,15 +247,35 @@
     nsend[1] = size
     for o in range(1, 16):
         norm_copy(1, o).start()
-    block(right_grams)
+    def right_side():
+        right_grams()
+        for t in range(4):
+            base = (left if t % 2 == 0 else right)[t // 2] + EPSILON * ident
+            gram = mats[t]
+            for part, term in enumerate((base * base, 2.0 * base * gram, gram * gram)):
+                frob[t, part] = jnp.broadcast_to(jnp.sum(term, keepdims=True), (8, 128))
+
+    block(right_side)
     norm_all(1).wait()
     for o in range(15):
         size = size + nrecv[1, o]
     norm_sq = jnp.sum(size, keepdims=True)
     clip = jnp.minimum(1.0, CLIP_NORM / (jnp.sqrt(norm_sq) + EPSILON))
 
-    ident = eye()
     fourths, factors = [], []
+
+    def near(cur):
+        return (0.25 * cur).astype(bf16)
+
+    def squared(n):
+        return 1.5625 * ident - 2.5 * n.astype(f32) + dot(n, n)
+
+    def advance_near(k, left_n, right_n):
+        y = roots[k]
+        high, low = split(y)
+        y = 1.25 * y - (dot(left_n, high) + dot(left_n, low))
+        high, low = split(y)
+        roots[k] = 1.25 * y - (dot(high, right_n) + dot(low, right_n))
 
     def advance(k, left_factor, right_factor):
         roots[k] = mm(split(mm(left_factor, split(roots[k]))), right_factor)
@@ -263,26 +284,33 @@
         for s in range(2):
             stats = left if s == 0 else right
             t = 2 * k + s
-            a = stats[k] + (clip * clip) * mats[t] + EPSILON * ident
-            zeta = 2.5 / jnp.sqrt(jnp.sum(a * a, keepdims=True))
+            clip2 = clip * clip
+            a = stats[k] + clip2 * mats[t] + EPSILON * ident
+            parts = [frob[t, part, 0:1, 0:1] for part in range(3)]
+            zeta = 2.5 / jnp.sqrt(parts[0] + clip2 * (parts[1] + clip2 * parts[2]))
             cur = zeta * a
-            p = 1.25 * ident - 0.25 * cur
             fourths.append(jnp.sqrt(jnp.sqrt(zeta)))
-            ps = split(p)
-            factors.append(ps)
-            ss = split(mm(ps, ps))
+            n = near(cur)
+            factors.append(n)
+            ss = split(squared(n))
             mats[t] = mm(split(mm(ss, split(cur))), ss)
 
     for k in range(2):
         roots[k] = (clip * fourths[2 * k] * fourths[2 * k + 1]) * summed[k]
-        advance(k, factors[2 * k], factors[2 * k + 1])
-
-    for _ in range(ITERS - 2):
+        advance_near(k, factors[2 * k], factors[2 * k + 1])
+
+    ada_sizes = []
+    for k in range(2):
+        g = clip * summed[k]
+        ada = g / (jnp.sqrt(accum[k] + g * g) + EPSILON)
+        ada_sizes.append(jnp.sqrt(jnp.sum(ada * ada, keepdims=True)))
+
+    for sweep in range(ITERS - 2):
         curs = [mats[t] for t in range(4)]
-        pss = [split(1.25 * ident - 0.25 * cur) for cur in curs]
-        sss = [split(mm(p, p)) for p in pss]
-        for k in range(2):
-            advance(k, pss[2 * k], pss[2 * k + 1])
+        ns = [near(cur) for cur in curs]
+        sss = [split(squared(n)) for n in ns]
+        for k in range(2):
+            advance_near(k, ns[2 * k], ns[2 * k + 1])
         uss = [split(mm(p, split(cur))) for p, cur in zip(sss, curs)]
         for t in range(4):
             mats[t] = mm(uss[t], sss[t])
@@ -291,12 +319,9 @@
         advance(k, *(split(1.25 * ident - 0.25 * mats[t]) for t in (2 * k, 2 * k + 1)))
 
     def finish(k):
-        g = clip * summed[k]
         sham = roots[k]
-        ada = g / (jnp.sqrt(accum[k] + g * g) + EPSILON)
-        ada_size = jnp.sqrt(jnp.sum(ada * ada, keepdims=True))
         sham_size = jnp.sqrt(jnp.sum(sham * sham, keepdims=True))
-        step = sham * (ada_size / (sham_size + EPSILON))
+        step = sham * (ada_sizes[k] / (sham_size + EPSILON))
         steps[k] = step
         ag[4 * z + 2 * c + k] = (master[k] - STEP_RATE * step).astype(bf16)
 
@@ -330,6 +355,9 @@
     def mate_out(k):
         own_share(k).wait_recv()
         ag_copy(1, k).start()
+
+    def drain(ref, sem):
+        pltpu.make_async_copy(ref, ref, sem).wait()
 
     last_factors(0)
     finish(0)
@@ -339,6 +367,13 @@
     block(lambda: finish(1))
     own_out(1)
     mate_out(1)
+    drain(stage, sib_ssem)
+    drain(sendq, q_ssem)
+    for j in range(7):
+        for k in range(2):
+            scale_copy(j, k).wait_send()
+    for stg in range(2):
+        drain(nrecv.at[stg], n_ssem.at[stg])
     for i in range(7):
         for k in range(2):
             ag_copy(i, k, 0).wait_recv()
@@ -346,18 +381,8 @@
                 ag_copy(i + 2, k).start()
             share(i, k).start()
 
-    def drain(ref, sem):
-        pltpu.make_async_copy(ref, ref, sem).wait()
-
-    drain(stage, sib_ssem)
-    drain(sendq, q_ssem)
     drain(ag.at[pl.ds(0, 14)], ag_ssem)
     drain(ag.at[pl.ds(0, 16)], x_ssem)
-    for j in range(7):
-        for k in range(2):
-            scale_copy(j, k).wait_send()
-    for stg in range(2):
-        drain(nrecv.at[stg], n_ssem.at[stg])
     drain(ag.at[pl.ds(0, 14)], x_rsem)
 
 
@@ -404,6 +429,7 @@
             pltpu.VMEM((2, 15, 8, 128), f32),
             pltpu.VMEM((4, W, W), f32),
             pltpu.VMEM(tiles, f32),
+            pltpu.VMEM((4, 3, 8, 128), f32),
             dma((6,)), pltpu.SemaphoreType.REGULAR((3,)), dma, dma((8,)), dma, dma((7, 2)), dma((7, 2)), dma((7, 2)),
             dma((2,)), dma((2,)), dma, dma((7, 2)), dma, dma, dma((2,)),
         ],

time: 85.1 us -> 82.7 us (0.972)
  Pallas kernels: 84.1 us -> 81.8 us
    pallas_call x1, Pallas kernels: 81.4 us -> 79.1 us  [per_device(): pl.pallas_call(kernel, out_shape=(pltpu.VMEM(tiles, f32), pltpu.VMEM((32,...]
where the time goes in v4:
time: 82.7 us; the launch traced here: 82.6 us
  Pallas kernels  81.8 us (99%)
    pallas_call x1, Pallas kernels, per_device(): pl.pallas_call(kernel, out_shape=(pltpu.VMEM(tiles, f32), pltpu.VMEM((32,...  79.1 us
    pallas_call x1, Pallas kernels, per_device(): pl.pallas_call(place, out_shape=(jax.ShapeDtypeStruct(band.shape, bf16),...  2.73 us

profile of v4, /device:TPU:1, one launch (start us, length us, event | category | flops | bytes accessed | tf_op | source)
XLA Modules:
  0.0 82.6 jit_solution(3924039201455119984)
XLA Ops:
  0.6 0.0 copy-start
  0.6 79.1 %shampoo.1 = (f32[2,256,256]{2,1,0:T(8,128)S(1)}, bf16[32,256,256]{2,1,0:T(8,128)(2,1)S(1)}) custom-call(s32[32]{0:T(128)} %table.1, bf16[512,4096]{1,0:T(8,128)(2,1)} %bitcast.1, f32[2,256,256]{2,1,0:T(8,128)} %left_h.1, f32[2,256,256]{2,1,0:T(8,128)} %right_h.1, f32[2,256,256]{2,1,0:T(8,128)} %accum_h.1, f32[2,256,256]{2,1,0:T(8,128)} %master_h.1), custom_call_target="tpu_custom_call" | custom-call | tf_op jit(solution)/shard_map/shampoo/pallas_call | solution.py:408
  79.7 0.0 copy-done
  79.7 2.7 %place.1 = (bf16[512,4096]{1,0:T(8,128)(2,1)}, f32[2,256,256]{2,1,0:T(8,128)}) custom-call(s32[32]{0:T(128)S(1)} %copy-done, bf16[32,256,256]{2,1,0:T(8,128)(2,1)S(1)} %get-tuple-element.6.gath, f32[2,256,256]{2,1,0:T(8,128)S(1)} %get-tuple-element.7.steps_in), custom_call_target="tpu_custom_call" | custom-call | tf_op jit(solution)/shard_map/place/pallas_call | solution.py:441
Async XLA Ops:
  0.6 79.1 %copy-start = (s32[32]{0:T(128)S(1)}, s32[32]{0:T(128)}, u32[]{:S(2)}) copy-start(s32[32]{0:T(128)} %table.1) | copy-start | bytes 388

commit v5 on v4

--- a/solution.py
+++ b/solution.py
@@ -131,22 +131,23 @@
     for load in loads[32:]:
         load.start()
 
-    def to_mate(j):
-        return pltpu.make_async_remote_copy(
-            src_ref=stage.at[j], dst_ref=sib.at[j], send_sem=sib_ssem, recv_sem=sib_rsem.at[j],
+    def to_mate(j, k):
+        half = pl.ds(k * W, W)
+        return pltpu.make_async_remote_copy(
+            src_ref=stage.at[j, half], dst_ref=sib.at[j, half], send_sem=sib_ssem, recv_sem=sib_rsem.at[j, k],
             device_id=mate, device_id_type=MESH,
         )
 
-    def fill(j):
+    def fill(j, k):
         hops, other = RS_ORDER[j]
-        for k in range(2):
-            stage[j, pl.ds(k * W, W), :] = band[table[4 * chip(-hops) + 2 * core(1 - other) + k]]
+        stage[j, pl.ds(k * W, W), :] = band[table[4 * chip(-hops) + 2 * core(1 - other) + k]]
 
     for j in range(8):
-        fill(j)
-        if j == 0:
-            pl.semaphore_wait(barrier, 8)
-        to_mate(j).start()
+        for k in range(2):
+            fill(j, k)
+            if j == 0 and k == 0:
+                pl.semaphore_wait(barrier, 8)
+            to_mate(j, k).start()
 
     def pair(j, k, i, ident):
         own = band[ident, pl.ds(32 * i, 32), :].astype(f32)
@@ -194,15 +195,16 @@
 
     tell(0)
     for j in range(7):
-        to_mate(j).wait_recv()
-        for k in range(2):
+        for k in range(2):
+            to_mate(j, k).wait_recv()
             message(j, k)
         if j in (2, 4, 6):
             turn = j // 2 - 1
             pl.semaphore_wait(near_sem.at[turn], 4)
             if turn < 2:
                 tell(turn + 1)
-    to_mate(7).wait_recv()
+    for k in range(2):
+        to_mate(7, k).wait_recv()
     size = jnp.zeros((8, 128), f32)
     for k in range(2):
         ident = table[4 * z + 2 * c + k]
@@ -305,15 +307,21 @@
         ada = g / (jnp.sqrt(accum[k] + g * g) + EPSILON)
         ada_sizes.append(jnp.sqrt(jnp.sum(ada * ada, keepdims=True)))
 
-    for sweep in range(ITERS - 2):
-        curs = [mats[t] for t in range(4)]
-        ns = [near(cur) for cur in curs]
-        sss = [split(squared(n)) for n in ns]
-        for k in range(2):
+    def sweep(group):
+        ts = [t for k in group for t in (2 * k, 2 * k + 1)]
+        curs = {t: mats[t] for t in ts}
+        ns = {t: near(curs[t]) for t in ts}
+        sss = {t: split(squared(ns[t])) for t in ts}
+        for k in group:
             advance_near(k, ns[2 * k], ns[2 * k + 1])
-        uss = [split(mm(p, split(cur))) for p, cur in zip(sss, curs)]
-        for t in range(4):
+        uss = {t: split(mm(sss[t], split(curs[t]))) for t in ts}
+        for t in ts:
             mats[t] = mm(uss[t], sss[t])
+
+    for _ in range(ITERS - 4):
+        sweep((0, 1))
+    for _ in range(2):
+        sweep((0,))
 
     def last_factors(k):
         advance(k, *(split(1.25 * ident - 0.25 * mats[t]) for t in (2 * k, 2 * k + 1)))
@@ -362,8 +370,15 @@
     last_factors(0)
     finish(0)
     own_out(0)
-    block(lambda: last_factors(1))
+
+    block(lambda: sweep((1,)))
     mate_out(0)
+
+    def second():
+        sweep((1,))
+        last_factors(1)
+
+    block(second)
     block(lambda: finish(1))
     own_out(1)
     mate_out(1)
@@ -430,7 +445,7 @@
             pltpu.VMEM((4, W, W), f32),
             pltpu.VMEM(tiles, f32),
             pltpu.VMEM((4, 3, 8, 128), f32),
-            dma((6,)), pltpu.SemaphoreType.REGULAR((3,)), dma, dma((8,)), dma, dma((7, 2)), dma((7, 2)), dma((7, 2)),
+            dma((6,)), pltpu.SemaphoreType.REGULAR((3,)), dma, dma((8, 2)), dma, dma((7, 2)), dma((7, 2)), dma((7, 2)),
             dma((2,)), dma((2,)), dma, dma((7, 2)), dma, dma, dma((2,)),
         ],
         compiler_params=pltpu.CompilerParams(

time: 82.7 us -> 81.5 us (0.985)
  Pallas kernels: 81.8 us -> 80.5 us
    pallas_call x1, Pallas kernels: 79.1 us -> 77.8 us  [per_device(): pl.pallas_call(kernel, out_shape=(pltpu.VMEM(tiles, f32), pltpu.VMEM((32,...]
where the time goes in v5:
time: 81.5 us; the launch traced here: 81.4 us
  Pallas kernels  80.5 us (99%)
  between operations  0.82 us (1%)
    pallas_call x1, Pallas kernels, per_device(): pl.pallas_call(kernel, out_shape=(pltpu.VMEM(tiles, f32), pltpu.VMEM((32,...  77.8 us
    pallas_call x1, Pallas kernels, per_device(): pl.pallas_call(place, out_shape=(jax.ShapeDtypeStruct(band.shape, bf16),...  2.73 us

profile of v5, /device:TPU:1, one launch (start us, length us, event | category | flops | bytes accessed | tf_op | source)
XLA Modules:
  0.0 81.4 jit_solution(3841519048845772394)
XLA Ops:
  0.6 0.0 copy-start
  0.6 77.8 %shampoo.1 = (f32[2,256,256]{2,1,0:T(8,128)S(1)}, bf16[32,256,256]{2,1,0:T(8,128)(2,1)S(1)}) custom-call(s32[32]{0:T(128)} %table.1, bf16[512,4096]{1,0:T(8,128)(2,1)} %bitcast.1, f32[2,256,256]{2,1,0:T(8,128)} %left_h.1, f32[2,256,256]{2,1,0:T(8,128)} %right_h.1, f32[2,256,256]{2,1,0:T(8,128)} %accum_h.1, f32[2,256,256]{2,1,0:T(8,128)} %master_h.1), custom_call_target="tpu_custom_call" | custom-call | tf_op jit(solution)/shard_map/shampoo/pallas_call | solution.py:423
  78.5 0.0 copy-done
  78.5 2.7 %place.1 = (bf16[512,4096]{1,0:T(8,128)(2,1)}, f32[2,256,256]{2,1,0:T(8,128)}) custom-call(s32[32]{0:T(128)S(1)} %copy-done, bf16[32,256,256]{2,1,0:T(8,128)(2,1)S(1)} %get-tuple-element.6.gath, f32[2,256,256]{2,1,0:T(8,128)S(1)} %get-tuple-element.7.steps_in), custom_call_target="tpu_custom_call" | custom-call | tf_op jit(solution)/shard_map/place/pallas_call | solution.py:456
Async XLA Ops:
  0.6 77.8 %copy-start = (s32[32]{0:T(128)S(1)}, s32[32]{0:T(128)}, u32[]{:S(2)}) copy-start(s32[32]{0:T(128)} %table.1) | copy-start | bytes 388
